TPU v7x, 256 devices: a whole 4x4x8 slice. The times are simulated.
256 devices in a mesh: row: 16 (over z_hi, x), col: 16 (over y, z_lo, core).
Axes of the slice: x: 4, y: 4, z: 8 (z_hi: 4, z_lo: 2; z = z_hi * 2 + z_lo), core: 2. Of those that a mesh axis runs over, the one named last changes fastest.
Arguments:
- matrix: bfloat16 [2, 4096, 40, 4096], P(None, 'row', None, 'col'), may hold values from -0.015625 to 0.015625
- diagonal: float32 [4096, 40], P(('col', 'row')), may hold values from 2.5 to 5
- right_side: float32 [4096, 40, 64], P(('col', 'row')), may hold values from -6 to 6
- slab_first: int32 [1], replicated, may hold values from 0 to 608
Outputs:
- solution: float32 [4096, 40, 64], P(('col', 'row'))
- residual: float32 [4096, 40, 64], P(('col', 'row'))
All inputs are finite; a program needn't handle non-finite values.
Results may differ from a plain program's by a relative error of at most 0.04.
Values may be sent and summed in bfloat16 or wider, within the bound.
A program may use at most 128 MiB of HBM per device.

v0:
```python
import jax
import jax.numpy as jnp
from jax import lax
from jax.sharding import PartitionSpec as P

ITERS = 3


def squares(residual):
    return lax.psum(jnp.sum(residual * residual, axis=(0, 1)), ("row", "col"))


def body(matrix, diagonal, right_side, slab_first):
    row_count = lax.axis_size("row")
    col_count = lax.axis_size("col")
    row_place = lax.axis_index("row")
    col_place = lax.axis_index("col")
    block_rows = matrix.shape[0]
    col_blocks = matrix.shape[2]
    global_rows = slab_first[0] + jnp.arange(block_rows, dtype=jnp.int32) * row_count + row_place
    block_cols = jnp.arange(col_blocks, dtype=jnp.int32) * col_count + col_place
    lower = block_cols[None, :] < global_rows[:, None]
    onblock = block_cols[None, :] == global_rows[:, None]
    weights = jnp.where(lower, 1.0, jnp.where(onblock, 0.5, 0.0)).astype(jnp.float32)
    owning_part = onblock.astype(jnp.float32)
    owning_half = owning_part.astype(jnp.bfloat16)
    weight_half = weights.astype(jnp.bfloat16)
    solution = jnp.zeros_like(right_side)
    residual = right_side
    direction = right_side
    norm_now = squares(residual)
    for step in range(ITERS):
        vector = direction
        column_entries = lax.all_gather(vector.astype(jnp.bfloat16), "row", axis=0, tiled=True)
        selected_rows = jnp.einsum(
            "jp,vpl->jvl", owning_half, column_entries, preferred_element_type=jnp.float32
        )
        slab_direction = lax.psum(selected_rows.astype(jnp.bfloat16), "col")
        masked = weight_half[:, None, :, None] * column_entries[None]
        row_part = jnp.einsum("arbc,acbn->arn", matrix, masked, preferred_element_type=jnp.float32)
        row_total_sum = lax.psum(row_part, "col")
        total = jnp.zeros(
            (lax.axis_size("row") * vector.shape[0], col_blocks, vector.shape[2]), jnp.float32
        )
        for index_position in range(block_rows):
            part = jnp.einsum(
                "vjx,vo->xjo",
                matrix[index_position],
                slab_direction[index_position],
                preferred_element_type=jnp.float32,
            )
            total = total + part * weights[index_position][None, :, None]
        offdiag = lax.psum_scatter(total, "row", scatter_dimension=0, tiled=True)
        positioned_rows = jnp.einsum(
            "rs,ril->isl", owning_part, row_total_sum, precision=lax.Precision.HIGHEST
        )
        offdiag = offdiag + lax.psum_scatter(
            positioned_rows, "row", scatter_dimension=0, tiled=True
        )
        image = diagonal[:, :, None] * vector + offdiag
        curve = lax.psum(jnp.sum(direction * image, axis=(0, 1)), ("row", "col"))
        step_length = norm_now / curve
        solution = solution + step_length * direction
        residual = residual - step_length * image
        norm_next = squares(residual)
        direction = residual + norm_next / norm_now * direction
        norm_now = norm_next
    return (solution, residual)


def solution(mesh):
    placed = (
        P(None, "row", None, "col"),
        P(("col", "row"), None),
        P(("col", "row"), None, None),
        P(),
    )
    return jax.shard_map(
        body,
        mesh=mesh,
        in_specs=placed,
        out_specs=(P(("col", "row"), None, None), P(("col", "row"), None, None)),
        check_vma=False,
    )
```

profile of v0, /device:TPU:1, one launch (start us, length us, event | category | flops | bytes accessed | tf_op | source)
XLA Modules:
  0.0 1652.4 jit_solution(6815870883992899405)
XLA Ops:
  7.2 1.7 convert_element_type.33
  9.6 10.5 copy.85
  20.2 57.6 %all-gather.4.cloned.1.call-done = bf16[256,40,64]{2,1,0:T(8,128)(2,1)} async-done(((bf16[16,40,64]{2,1,0:T(8,128)(2,1)}), bf16[256,40,64]{2,1,0:T(8,128)(2,1)}) %all-gather.4.cloned.1.call-update) | async-done | bytes 1310736 | tf_op jit(solution)/shard_map/all_gather | solution.py:34
  77.9 5.9 copy.84
  83.8 4.2 convolution_convert_fusion.2
  88.1 3.5 copy.87
  91.6 6.8 fusion.18
  98.5 97.2 %all-reduce.8.cloned.1.call-done = bf16[2,256,64]{1,0,2:T(2,128)(2,1)} async-done(((bf16[2,256,64]{1,0,2:T(2,128)(2,1)}), bf16[2,256,64]{1,0,2:T(2,128)(2,1)}) %all-reduce.8.cloned.1.call-update) | async-done | bytes 65552 | tf_op jit(solution)/shard_map/psum | solution.py:38
  196.7 3.5 fusion.2
  200.3 119.1 %all-reduce.10.cloned.1.call-done = f32[2,256,64]{1,2,0:T(8,128)} async-done(((f32[2,256,64]{1,2,0:T(8,128)}), f32[2,256,64]{1,2,0:T(8,128)}) %all-reduce.10.cloned.1.call-update) | async-done | bytes 131088 | tf_op jit(solution)/shard_map/psum | solution.py:41
  319.3 2.2 fusion.31
  321.5 5.4 bitcast_add_fusion.2
  326.9 6.0 copy.91
  333.0 100.7 %reduce-scatter.4.cloned.1.call-done = f32[16,40,64]{2,1,0:T(8,128)} async-done(((f32[256,40,64]{2,1,0:T(8,128)}), f32[16,40,64]{2,1,0:T(8,128)}) %reduce-scatter.4.cloned.1.call-update) | async-done | bytes 163856 | tf_op jit(solution)/shard_map/reduce_scatter | solution.py:53
  433.7 1.1 multiply_reduce_fusion.4
  434.8 75.9 %all-reduce = (f32[64]{0:T(128)S(1)}, f32[64]{0:T(128)S(1)}) all-reduce(f32[64]{0:T(128)S(1)} %get-tuple-element.7, f32[64]{0:T(128)S(1)} %get-tuple-element.6), channel_id=1, replica_groups=mesh['row'=16,'col'=16] {'row','col'}, use_global_device_ids=true, to_apply=%region_1.2 | all-reduce | flops 128 | bytes 1024 | tf_op jit(solution)/shard_map/psum | solution.py:10
  510.8 1.1 multiply_reduce_fusion.3
  511.9 72.6 %psum.88 = f32[64]{0:T(128)S(1)} all-reduce(f32[64]{0:T(128)S(1)} %multiply_reduce_fusion.3), channel_id=1, replica_groups=mesh['row'=16,'col'=16] {'row','col'}, use_global_device_ids=true, to_apply=%region_9.10 | all-reduce | flops 64 | bytes 512 | tf_op jit(solution)/shard_map/psum | solution.py:10
  584.5 1.8 fusion.55
  586.3 58.8 %all-gather.6.cloned.1.call-done = bf16[256,40,64]{2,1,0:T(8,128)(2,1)} async-done(((bf16[16,40,64]{2,1,0:T(8,128)(2,1)}), bf16[256,40,64]{2,1,0:T(8,128)(2,1)}) %all-gather.6.cloned.1.call-update) | async-done | bytes 1310736 | tf_op jit(solution)/shard_map/all_gather | solution.py:34
  645.1 5.9 copy.92
  651.0 4.2 convolution_convert_fusion.1
  655.3 3.5 copy.93
  658.8 6.8 fusion.21
  665.7 97.2 %all-reduce.12.cloned.1.call-done = bf16[2,256,64]{1,0,2:T(2,128)(2,1)} async-done(((bf16[2,256,64]{1,0,2:T(2,128)(2,1)}), bf16[2,256,64]{1,0,2:T(2,128)(2,1)}) %all-reduce.12.cloned.1.call-update) | async-done | bytes 65552 | tf_op jit(solution)/shard_map/psum | solution.py:38
  764.0 3.5 fusion.1
  767.5 119.0 %all-reduce.14.cloned.1.call-done = f32[2,256,64]{1,2,0:T(8,128)} async-done(((f32[2,256,64]{1,2,0:T(8,128)}), f32[2,256,64]{1,2,0:T(8,128)}) %all-reduce.14.cloned.1.call-update) | async-done | bytes 131088 | tf_op jit(solution)/shard_map/psum | solution.py:41
  886.5 2.2 fusion.29
  888.7 5.4 bitcast_add_fusion.1
  894.2 6.0 copy.97
  900.2 100.4 %reduce-scatter.6.cloned.1.call-done = f32[16,40,64]{2,1,0:T(8,128)} async-done(((f32[256,40,64]{2,1,0:T(8,128)}), f32[16,40,64]{2,1,0:T(8,128)}) %reduce-scatter.6.cloned.1.call-update) | async-done | bytes 163856 | tf_op jit(solution)/shard_map/reduce_scatter | solution.py:53
  1001.8 75.9 %psum.91 = f32[64]{0:T(128)S(1)} all-reduce(f32[64]{0:T(128)S(1)} %multiply_reduce_fusion.2), channel_id=1, replica_groups=mesh['row'=16,'col'=16] {'row','col'}, use_global_device_ids=true, to_apply=%region_15.16 | all-reduce | flops 64 | bytes 512 | tf_op jit(solution)/shard_map/psum | solution.py:61
  1077.7 1.2 multiply_reduce_fusion.1
  1078.9 72.4 %psum.92 = f32[64]{0:T(128)S(1)} all-reduce(f32[64]{0:T(128)S(1)} %get-tuple-element.10), channel_id=1, replica_groups=mesh['row'=16,'col'=16] {'row','col'}, use_global_device_ids=true, to_apply=%region_17.18 | all-reduce | flops 64 | bytes 512 | tf_op jit(solution)/shard_map/psum | solution.py:10
  1152.1 58.9 %all-gather.8.cloned.1.call-done = bf16[256,40,64]{2,1,0:T(8,128)(2,1)} async-done(((bf16[16,40,64]{2,1,0:T(8,128)(2,1)}), bf16[256,40,64]{2,1,0:T(8,128)(2,1)}) %all-gather.8.cloned.1.call-update) | async-done | bytes 1310736 | tf_op jit(solution)/shard_map/all_gather | solution.py:34
  1211.0 5.9 copy.98
  1216.9 4.2 convolution_convert_fusion
  1221.4 3.5 copy.99
  1224.9 6.8 fusion.24
  1231.8 97.0 %all-reduce.16.cloned.1.call-done = bf16[2,256,64]{1,0,2:T(2,128)(2,1)} async-done(((bf16[2,256,64]{1,0,2:T(2,128)(2,1)}), bf16[2,256,64]{1,0,2:T(2,128)(2,1)}) %all-reduce.16.cloned.1.call-update) | async-done | bytes 65552 | tf_op jit(solution)/shard_map/psum | solution.py:38
  1329.9 3.5 fusion
  1333.4 119.1 %all-reduce.18.cloned.1.call-done = f32[2,256,64]{1,2,0:T(8,128)} async-done(((f32[2,256,64]{1,2,0:T(8,128)}), f32[2,256,64]{1,2,0:T(8,128)}) %all-reduce.18.cloned.1.call-update) | async-done | bytes 131088 | tf_op jit(solution)/shard_map/psum | solution.py:41
  1452.4 2.2 fusion.27
  1454.6 5.5 bitcast_add_fusion
  1460.1 6.1 copy.103
  1466.2 100.4 %reduce-scatter.8.cloned.1.call-done = f32[16,40,64]{2,1,0:T(8,128)} async-done(((f32[256,40,64]{2,1,0:T(8,128)}), f32[16,40,64]{2,1,0:T(8,128)}) %reduce-scatter.8.cloned.1.call-update) | async-done | bytes 163856 | tf_op jit(solution)/shard_map/reduce_scatter | solution.py:53
  1567.7 75.9 %psum.95 = f32[64]{0:T(128)S(1)} all-reduce(f32[64]{0:T(128)S(1)} %multiply_reduce_fusion), channel_id=1, replica_groups=mesh['row'=16,'col'=16] {'row','col'}, use_global_device_ids=true, to_apply=%region_23.24 | all-reduce | flops 64 | bytes 512 | tf_op jit(solution)/shard_map/psum | solution.py:61
  1643.6 1.9 multiply_subtract_fusion
  (55 shorter events, 7.1 us)
Async XLA Ops:
  7.2 70.7 %all-gather.4.cloned.1.call-start = ((), (), s32[]{:S(2)}) async-start(), calls=%async_computation.3 | async-start | bytes 2785280 | tf_op jit(solution)/shard_map/all_gather | solution.py:34
  8.9 186.8 %all-reduce.8.cloned.1.call-start = ((), (), s32[]{:S(2)}) async-start(), calls=%async_computation.4 | async-start | bytes 131072 | tf_op jit(solution)/shard_map/psum | solution.py:38
  83.8 4.3 copy-start.1
  88.0 231.3 %all-reduce.10.cloned.1.call-start = ((), (), s32[]{:S(2)}) async-start(), calls=%async_computation.5 | async-start | bytes 262144 | tf_op jit(solution)/shard_map/psum | solution.py:41
  98.4 335.3 %reduce-scatter.4.cloned.1.call-start = ((), (), s32[]{:S(2)}) async-start(), calls=%async_computation.12 | async-start | bytes 5570560 | tf_op jit(solution)/shard_map/reduce_scatter | solution.py:53
  332.9 100.8 %copy-start = (f32[16,40,64]{2,1,0:T(8,128)S(1)}, f32[16,40,64]{2,1,0:T(8,128)}, u32[]{:S(2)}) copy-start(f32[16,40,64]{2,1,0:T(8,128)} %param.6) | copy-start | bytes 491524
  332.9 100.8 %copy-start.7 = (f32[16,40]{1,0:T(8,128)S(1)}, f32[16,40]{1,0:T(8,128)}, u32[]{:S(2)}) copy-start(f32[16,40]{1,0:T(8,128)} %param.5) | copy-start | bytes 7684
  333.0 312.1 %all-gather.6.cloned.1.call-start = ((), (), s32[]{:S(2)}) async-start(), calls=%async_computation.6 | async-start | bytes 2785280 | tf_op jit(solution)/shard_map/all_gather | solution.py:34
  586.3 176.6 %all-reduce.12.cloned.1.call-start = ((), (), s32[]{:S(2)}) async-start(), calls=%async_computation.7 | async-start | bytes 131072 | tf_op jit(solution)/shard_map/psum | solution.py:38
  651.0 4.3 copy-start.2
  655.3 231.3 %all-reduce.14.cloned.1.call-start = ((), (), s32[]{:S(2)}) async-start(), calls=%async_computation.8 | async-start | bytes 262144 | tf_op jit(solution)/shard_map/psum | solution.py:41
  665.7 335.0 %reduce-scatter.6.cloned.1.call-start = ((), (), s32[]{:S(2)}) async-start(), calls=%async_computation.13 | async-start | bytes 5570560 | tf_op jit(solution)/shard_map/reduce_scatter | solution.py:53
  900.2 177.6 %copy-start.6 = (f32[16,40,64]{2,1,0:T(8,128)S(1)}, f32[16,40,64]{2,1,0:T(8,128)}, u32[]{:S(2)}) copy-start(f32[16,40,64]{2,1,0:T(8,128)} %reduce-scatter.4.cloned.1.call-done) | copy-start | bytes 491524
  900.2 310.8 %all-gather.8.cloned.1.call-start = ((), (), s32[]{:S(2)}) async-start(), calls=%async_computation.9 | async-start | bytes 2785280 | tf_op jit(solution)/shard_map/all_gather | solution.py:34
  1078.9 132.1 %copy-start.4 = (f32[16,40,64]{2,1,0:T(8,128)}, f32[16,40,64]{2,1,0:T(8,128)S(1)}, u32[]{:S(2)}) copy-start(f32[16,40,64]{2,1,0:T(8,128)S(1)} %get-tuple-element.11) | copy-start | bytes 491524
  1152.0 176.8 %all-reduce.16.cloned.1.call-start = ((), (), s32[]{:S(2)}) async-start(), calls=%async_computation.10 | async-start | bytes 131072 | tf_op jit(solution)/shard_map/psum | solution.py:38
  1216.9 4.5 copy-start.3
  1221.1 231.3 %all-reduce.18.cloned.1.call-start = ((), (), s32[]{:S(2)}) async-start(), calls=%async_computation.11 | async-start | bytes 262144 | tf_op jit(solution)/shard_map/psum | solution.py:41
  1231.8 334.8 %reduce-scatter.8.cloned.1.call-start = ((), (), s32[]{:S(2)}) async-start(), calls=%async_computation.14 | async-start | bytes 5570560 | tf_op jit(solution)/shard_map/reduce_scatter | solution.py:53
  1466.2 100.4 %copy-start.5 = (f32[16,40,64]{2,1,0:T(8,128)S(1)}, f32[16,40,64]{2,1,0:T(8,128)}, u32[]{:S(2)}) copy-start(f32[16,40,64]{2,1,0:T(8,128)} %copy-done.4) | copy-start | bytes 491524
Sparse Core Ops, SparseCore 0:
  11.0 66.8 all-gather.3
  88.1 107.5 all-reduce.7
  199.1 120.1 all-reduce.9
  333.1 100.5 reduce-scatter.3
  586.4 58.6 all-gather.5
  655.4 107.5 all-reduce.11
  766.3 120.1 all-reduce.13
  900.3 100.3 reduce-scatter.5
  1152.2 58.7 all-gather.7
  1221.3 107.5 all-reduce.15
  1332.2 120.1 all-reduce.17
  1466.3 100.1 reduce-scatter.7
where the time goes:
time: 1650 us
  waiting for transfers between devices  1130 us (68%)
  blocking collectives  373 us (23%)
  matrix products  66.4 us (4%)
  local copies, waits for them, and re-layouts  60 us (4%)
    psum x3, waiting for transfers between devices, body(): row_total_sum = lax.psum(row_part, 'col')  357 us
    reduce_scatter x3, waiting for transfers between devices, body(): offdiag = lax.psum_scatter(total, 'row', scatter_dimension=0, tiled=True)  301 us
    psum x3, waiting for transfers between devices, body(): slab_direction = lax.psum(selected_rows.astype(jnp.bfloat16), 'col')  291 us
    psum x3, blocking collectives, squares(): return lax.psum(jnp.sum(residual * residual, axis=(0, 1)), ('row', 'col'))  221 us
    all_gather x3, waiting for transfers between devices, body(): lax.all_gather(vector.astype(jnp.bfloat16), 'row', axis=0, tiled=True)  175 us
    psum x2, blocking collectives, body(): curve = lax.psum(jnp.sum(direction * image, axis=(0, 1)), ('row', 'col'))  152 us
  transfers between devices with their start and end apart: 12, of which 12 were waited for; matrix products, arithmetic and copies ran while one was open for 3% of the time, Pallas kernels for 0%

commit v1 on v0

v1 whole, which is shorter than its diff:
```python
import functools

import jax
import jax.numpy as jnp
from jax import lax
from jax.experimental import pallas as pl
from jax.experimental.pallas import tpu as pltpu
from jax.sharding import PartitionSpec as P

ITERS = 3
NX = 4
MESH = pl.DeviceIdType.MESH
F32 = jnp.float32
BF16 = jnp.bfloat16
LANES = 128
HALF = 64
CELLS = 16
MSG = CELLS + 8


def column_sums(values):
    total = jnp.sum(jnp.sum(values, axis=0), axis=0, keepdims=True)
    total = jnp.broadcast_to(total, (8, LANES))
    return total + pltpu.roll(total, HALF, 1)


def kernel(
    nx, nz,
    first_ref, matrix_hbm, diag_ref, right_ref,
    sol_ref, res_ref,
    matrix, gathered, mirror, got_x, sums_z, got_z,
    direction, image, slab_dir, slab_img, acc, norm_ref,
    out1, in1, out2, in2, out_a, in_a, out_b, in_b,
    load_sem, gz_send, gz_recv, gx_send, gx_recv,
    mx_send, mx_recv, mz_send, mz_recv, hop_send, hop_recv,
):
    n = nx * nz
    pairs = diag_ref.shape[0]
    order = n * CELLS
    i = lax.axis_index("row")
    j = lax.axis_index("col")
    z = i // nx
    x = i % nx
    first = first_ref[0]
    my_row = (j - first) & (n - 1)
    my_block = (first + my_row) // n
    my_col = (first + i) & (n - 1)
    odd = (my_block & 1) == 1

    load = pltpu.make_async_copy(matrix_hbm, matrix, load_sem)
    load.start()

    block_of = (
        2 * lax.broadcasted_iota(jnp.int32, (pairs, CELLS, LANES), 0)
        + lax.broadcasted_iota(jnp.int32, (pairs, CELLS, LANES), 2) // HALF
    )
    owned = (block_of == my_block) | (block_of == my_block + 1)
    slot_of = lax.broadcasted_iota(jnp.int32, (n, CELLS, LANES), 0)
    left_half = lax.broadcasted_iota(jnp.int32, (order, LANES), 1) < HALF
    even_lanes = (lax.broadcasted_iota(jnp.int32, (CELLS, LANES), 1) < HALF).astype(F32)
    even_mask = even_lanes.astype(BF16)
    odd_mask = (1.0 - even_lanes).astype(BF16)

    def swap(piece):
        return jnp.where(odd, pltpu.roll(piece, HALF, 1), piece)

    def row_copy(src, dst, send, recv, zz, xx):
        return pltpu.make_async_remote_copy(
            src_ref=src, dst_ref=dst, send_sem=send, recv_sem=recv,
            device_id=(zz * nx + xx, j), device_id_type=MESH,
        )

    def hop_copy(src, dst, k, h, row, col):
        return pltpu.make_async_remote_copy(
            src_ref=src, dst_ref=dst, send_sem=hop_send.at[k, h],
            recv_sem=hop_recv.at[k, h], device_id=(row, col), device_id_type=MESH,
        )

    sol_ref[...] = jnp.zeros_like(sol_ref)
    res_ref[...] = right_ref[...]
    direction[...] = jnp.zeros_like(direction)
    image[...] = jnp.zeros_like(image)
    slab_dir[...] = jnp.zeros_like(slab_dir)
    slab_img[...] = jnp.zeros_like(slab_img)
    norm_ref[...] = jnp.ones_like(norm_ref)

    def iteration(k, carry):
        residual = res_ref[...]
        gathered[k, z, x] = residual.astype(BF16)

        def spread_z(dz):
            return row_copy(
                gathered.at[k, z, x], gathered.at[k, z, x],
                gz_send.at[k, dz - 1], gz_recv.at[k, dz - 1], (z + dz) % nz, x,
            )

        def spread_x(dx, dz):
            zz = (z - dz + nz) % nz
            return row_copy(
                gathered.at[k, zz, x], gathered.at[k, zz, x],
                gx_send.at[k, dz, dx - 1], gx_recv.at[k, dz, dx - 1], z, (x + dx) % nx,
            )

        for dz in range(1, nz):
            spread_z(dz).start()

        piece = swap(jnp.sum(jnp.where(owned, residual, 0.0), axis=0))
        out1[k, 0:CELLS] = piece
        out1[k, CELLS:MSG] = column_sums(residual * residual)

        def hop1(step, c):
            row = (i + step) % n

            @pl.when((row != i) | (i != j))
            def _():
                hop_copy(out1.at[k], in1.at[k, j], k, 0, row, i).start()

            return c

        lax.fori_loop(0, n, hop1, 0)

        @pl.when(i == j)
        def _():
            in1[k, j] = out1[k]

        for dx in range(1, nx):
            spread_x(dx, 0).start()

        def hop_wait(buf, h, slots):
            hop_copy(buf.at[k, 0:slots], buf.at[k, 0:slots], k, h, i, j).wait()

        def wait_cross(buf, h):
            @pl.when(i == j)
            def _():
                hop_wait(buf, h, n - 1)

            @pl.when(i != j)
            def _():
                hop_wait(buf, h, n)

        wait_cross(in1, 0)
        piece = jnp.sum(jnp.where(slot_of == my_col, in1[k, :, 0:CELLS, :], 0.0), axis=0)
        sums = jnp.sum(in1[k, :, CELLS:MSG, :], axis=0)
        out2[k, 0:CELLS] = piece
        out2[k, CELLS:MSG] = sums
        in2[k, j] = out2[k]

        def hop2(step, c):
            hop_copy(out2.at[k], in2.at[k, j], k, 1, i, (j + step) % n).start()
            return c

        lax.fori_loop(1, n, hop2, 0)

        for dz in range(1, nz):
            spread_z(dz).wait()
            for dx in range(1, nx):
                spread_x(dx, dz).start()

        hop_wait(in2, 1, n - 1)
        slab = in2[k, :, 0:CELLS, :].reshape(order, LANES)
        norm = jnp.sum(in2[k, :, CELLS:MSG, :], axis=0)
        beta = jnp.where(k == 0, 0.0, norm / norm_ref[...])
        norm_ref[...] = norm
        beta_row = beta[0:1, :]
        slab_d = slab + beta_row * slab_dir[...]
        slab_dir[...] = slab_d
        beta_cell = beta_row.reshape(1, 1, LANES)
        cells_d = residual + beta_cell * direction[...]
        direction[...] = cells_d

        @pl.when(k == 0)
        def _():
            load.wait()

        turned = jnp.transpose(slab).astype(BF16)
        both = jnp.concatenate([turned[0:HALF], turned[HALF:LANES]], axis=1)

        def transposed(p, c):
            parts = [
                jnp.dot(both, matrix[2 * p + h], preferred_element_type=F32)
                for h in range(2)
            ]
            cells = jnp.transpose(jnp.concatenate(parts, axis=0))
            mirror[:, :, p] = cells.astype(BF16).reshape(nz, nx, CELLS, LANES)
            return c

        lax.fori_loop(0, pairs, transposed, 0)

        def mirror_x(dx):
            xx = (x + dx) % nx
            return row_copy(
                mirror.at[:, xx], got_x.at[k, dx - 1],
                mx_send.at[k, dx - 1], mx_recv.at[k, dx - 1], z, xx,
            )

        def mirror_z(dz):
            zz = (z + dz) % nz
            return row_copy(
                sums_z.at[zz], got_z.at[k, dz - 1],
                mz_send.at[k, dz - 1], mz_recv.at[k, dz - 1], zz, x,
            )

        for dx in range(1, nx):
            mirror_x(dx).start()

        for dz in range(nz):
            for dx in range(1, nx):
                spread_x(dx, dz).wait()

        acc[...] = jnp.zeros_like(acc)

        def forward(p, c):
            cells = gathered[k, :, :, p].reshape(n, CELLS, LANES)
            evens = (cells * even_mask).reshape(order, LANES)
            odds = (cells * odd_mask).reshape(order, LANES)
            acc[...] += jnp.dot(matrix[2 * p], evens, preferred_element_type=F32) + jnp.dot(
                matrix[2 * p + 1], odds, preferred_element_type=F32
            )
            return c

        lax.fori_loop(0, pairs, forward, 0)
        rows = acc[...]
        rows = rows + pltpu.roll(rows, HALF, 1)
        rows = jnp.where(left_half, rows[0:order], rows[order:])
        slab_q = rows + beta_row * slab_img[...]
        slab_img[...] = slab_q
        curve = column_sums(diag_ref[...] * cells_d * cells_d)
        curve = curve + 2.0 * column_sums((slab_d * slab_q).reshape(n, CELLS, LANES))

        out_a[k, :, 0:CELLS] = rows.reshape(n, CELLS, LANES)
        out_a[k, :, CELLS:MSG] = jnp.broadcast_to(curve, (n, 8, LANES))
        in_a[k, j] = out_a[k, j]

        def hop_a(step, c):
            col = (j + step) % n
            hop_copy(out_a.at[k, col], in_a.at[k, j], k, 2, i, col).start()
            return c

        lax.fori_loop(1, n, hop_a, 0)

        for dx in range(1, nx):
            mirror_x(dx).wait()
        for dz in range(nz):
            zz = (z + dz) % nz
            total = mirror[zz, x].astype(F32)
            for dx in range(1, nx):
                total = total + got_x[k, dx - 1, zz].astype(F32)
            sums_z[zz] = total.astype(BF16)
        for dz in range(1, nz):
            mirror_z(dz).start()

        hop_wait(in_a, 2, n - 1)
        out_b[k] = jnp.sum(in_a[k], axis=0)

        def hop_b(step, c):
            col = (j + step) % n

            @pl.when((col != j) | (i != j))
            def _():
                hop_copy(out_b.at[k], in_b.at[k, i], k, 3, j, col).start()

            return c

        lax.fori_loop(0, n, hop_b, 0)

        @pl.when(i == j)
        def _():
            in_b[k, i] = out_b[k]

        for dz in range(1, nz):
            mirror_z(dz).wait()
        applied = diag_ref[...] * residual + sums_z[z].astype(F32)
        for dz in range(1, nz):
            applied = applied + got_z[k, dz - 1].astype(F32)

        wait_cross(in_b, 3)
        piece = swap(
            jnp.sum(jnp.where(slot_of == my_row, in_b[k, :, 0:CELLS, :], 0.0), axis=0)
        )
        curve = jnp.sum(in_b[k, :, CELLS:MSG, :], axis=0)
        applied = applied + jnp.where(owned, piece.reshape(1, CELLS, LANES), 0.0)
        applied = applied + beta_cell * image[...]
        image[...] = applied
        length = (norm / curve)[0:1, :].reshape(1, 1, LANES)
        sol_ref[...] = sol_ref[...] + length * cells_d
        res_ref[...] = residual - length * applied
        return carry

    lax.fori_loop(0, ITERS, iteration, 0)


def body(nx, matrix, diagonal, right_side, slab_first):
    n = lax.axis_size("row")
    nz = n // nx
    rb, order, blocks, _ = matrix.shape
    cells, _, width = right_side.shape
    pairs = blocks // 2
    rows = slab_first[0] + jnp.arange(rb, dtype=jnp.int32) * n + lax.axis_index("row")
    cols = jnp.arange(blocks, dtype=jnp.int32) * n + lax.axis_index("col")
    weight = jnp.where(
        cols[:, None] < rows[None, :], 1.0, jnp.where(cols[:, None] == rows[None, :], 0.5, 0.0)
    ).astype(matrix.dtype)
    turned = jnp.transpose(matrix, (2, 0, 1, 3)) * weight[:, :, None, None]
    turned = turned.reshape(blocks, rb * order, order)

    def packed(cell_array):
        return jnp.transpose(cell_array.reshape(cells, pairs, LANES), (1, 0, 2))

    def unpacked(cell_array):
        return jnp.transpose(cell_array, (1, 0, 2)).reshape(cells, blocks, width)

    diag = packed(jnp.broadcast_to(diagonal[:, :, None], right_side.shape))
    vec = (pairs, cells, LANES)
    vmem = pl.BlockSpec(memory_space=pltpu.VMEM)
    dma = pltpu.SemaphoreType.DMA
    sol, res = pl.pallas_call(
        functools.partial(kernel, nx, nz),
        out_shape=[jax.ShapeDtypeStruct(vec, F32)] * 2,
        in_specs=[
            pl.BlockSpec(memory_space=pltpu.SMEM),
            pl.BlockSpec(memory_space=pl.ANY),
            vmem,
            vmem,
        ],
        out_specs=[vmem, vmem],
        scratch_shapes=[
            pltpu.VMEM((blocks, rb * order, order), BF16),
            pltpu.VMEM((ITERS, nz, nx) + vec, BF16),
            pltpu.VMEM((nz, nx) + vec, BF16),
            pltpu.VMEM((ITERS, nx - 1, nz) + vec, BF16),
            pltpu.VMEM((nz,) + vec, BF16),
            pltpu.VMEM((ITERS, nz - 1) + vec, BF16),
            pltpu.VMEM(vec, F32),
            pltpu.VMEM(vec, F32),
            pltpu.VMEM((order, LANES), F32),
            pltpu.VMEM((order, LANES), F32),
            pltpu.VMEM((rb * order, LANES), F32),
            pltpu.VMEM((8, LANES), F32),
            pltpu.VMEM((ITERS, MSG, LANES), F32),
            pltpu.VMEM((ITERS, n, MSG, LANES), F32),
            pltpu.VMEM((ITERS, MSG, LANES), F32),
            pltpu.VMEM((ITERS, n, MSG, LANES), F32),
            pltpu.VMEM((ITERS, n, MSG, LANES), F32),
            pltpu.VMEM((ITERS, n, MSG, LANES), F32),
            pltpu.VMEM((ITERS, MSG, LANES), F32),
            pltpu.VMEM((ITERS, n, MSG, LANES), F32),
            dma,
            dma((ITERS, nz - 1)),
            dma((ITERS, nz - 1)),
            dma((ITERS, nz, nx - 1)),
            dma((ITERS, nz, nx - 1)),
            dma((ITERS, nx - 1)),
            dma((ITERS, nx - 1)),
            dma((ITERS, nz - 1)),
            dma((ITERS, nz - 1)),
            dma((ITERS, 4)),
            dma((ITERS, 4)),
        ],
        compiler_params=pltpu.CompilerParams(
            has_side_effects=True, vmem_limit_bytes=48 * 1024 * 1024
        ),
        name="conjugate_gradients",
    )(slab_first, turned, diag, packed(right_side))
    return unpacked(sol), unpacked(res)


def solution(mesh, nx=NX):
    placed = (
        P(None, "row", None, "col"),
        P(("col", "row"), None),
        P(("col", "row"), None, None),
        P(),
    )
    return jax.shard_map(
        functools.partial(body, nx),
        mesh=mesh,
        in_specs=placed,
        out_specs=(P(("col", "row"), None, None), P(("col", "row"), None, None)),
        check_vma=False,
    )
```

time: 1650 us -> 248 us (0.15)
  waiting for transfers between devices: 1130 us -> 0 us
  blocking collectives: 373 us -> 0 us
  Pallas kernels: 0 us -> 223 us
  matrix products: 66.4 us -> 0 us
  local copies, waits for them, and re-layouts: 60 us -> 12.6 us
    psum x6 -> x0, waiting for transfers between devices: 649 us -> none  [the longest x3 357 us: body(): row_total_sum = lax.psum(row_part, 'col')]
    psum x5 -> x0, blocking collectives: 373 us -> none  [the longest x3 221 us: squares(): return lax.psum(jnp.sum(residual * residual, axis=(0, 1)), ('row', 'col'))]
    reduce_scatter x3 -> x0, waiting for transfers between devices: 301 us -> none  [body(): offdiag = lax.psum_scatter(total, 'row', scatter_dimension=0, tiled=True)]
    pallas_call x0 -> x1, Pallas kernels: none -> 223 us  [body(): pl.pallas_call(functools.partial(kernel, nx, nz), out_shape=[jax.ShapeDty...]
    all_gather x3 -> x0, waiting for transfers between devices: 175 us -> none  [body(): lax.all_gather(vector.astype(jnp.bfloat16), 'row', axis=0, tiled=True)]
    dot_general x15 -> x0, matrix products: 66.4 us -> none  [the longest x6 26.8 us: body(): jnp.einsum('vjx,vo->xjo', matrix[index_position], slab_direction[index_po...]
    all_gather x6 -> x0, local copies, waits for them, and re-layouts: 28.3 us -> none  [body(): lax.all_gather(vector.astype(jnp.bfloat16), 'row', axis=0, tiled=True)]
    add x3 -> x0, local copies, waits for them, and re-layouts: 18.1 us -> none  [body(): offdiag + lax.psum_scatter(positioned_rows, 'row', scatter_dimension=0, t...]
  transfers between devices with their start and end apart: 12 -> 0, of which waited for: 12 -> 0; matrix products, arithmetic and copies ran while one was open for 3% -> 0% of each run, Pallas kernels for 0% -> 0%
where the time goes in v1:
time: 248 us; the launch traced here: 246 us
  Pallas kernels  223 us (90%)
  local copies, waits for them, and re-layouts  12.6 us (5%)
  other arithmetic  8.77 us (4%)
    pallas_call x1, Pallas kernels, body(): pl.pallas_call(functools.partial(kernel, nx, nz), out_shape=[jax.ShapeDty...  223 us
    mul x1, local copies, waits for them, and re-layouts, body(): turned = jnp.transpose(matrix, (2, 0, 1, 3)) * weight[:, :, None, None]  10.4 us
    mul x1, other arithmetic, body(): turned = jnp.transpose(matrix, (2, 0, 1, 3)) * weight[:, :, None, None]  8.69 us

profile of v1, /device:TPU:1, one launch (start us, length us, event | category | flops | bytes accessed | tf_op | source)
XLA Modules:
  0.0 246.1 jit_solution(6131470909243088504)
XLA Ops:
  1.3 0.1 fusion
  1.4 8.7 %bitcast_multiply_fusion = bf16[40,2,256,256]{3,0,2,1:T(8,128)(2,1)} fusion(bf16[2,256,40,256]{3,2,1,0:T(8,128)(2,1)} %param.4, bf16[40,2]{0,1:T(2,128)(2,1)S(1)} %fusion), kind=kLoop, calls=%fused_computation | loop fusion | flops 5242880 | bytes 20971680 | tf_op jit(solution)/shard_map/mul | solution.py:303
  10.1 0.0 copy-start.1
  10.1 0.0 copy-start
  10.1 10.4 %copy.7 = bf16[40,2,256,256]{3,2,1,0:T(8,128)(2,1)} copy(bf16[40,2,256,256]{3,0,2,1:T(8,128)(2,1)} %bitcast_multiply_fusion) | data formatting | bytes 20971520 | tf_op jit(solution)/shard_map/mul | solution.py:303
  20.5 0.0 copy-done.1
  20.5 0.1 broadcast_in_dim.26
  20.6 0.1 reshape.89
  20.7 0.0 copy-done
  20.7 0.1 reshape.90
  20.8 0.1 copy_bitcast_fusion
  20.9 223.4 %conjugate_gradients.1 = (f32[20,16,128]{2,1,0:T(8,128)S(1)}, f32[20,16,128]{2,1,0:T(8,128)S(1)}) custom-call(s32[1]{0:T(128)} %copy.14.first_ref, bf16[40,512,256]{2,1,0:T(8,128)(2,1)} %bitcast.13, f32[20,16,128]{2,1,0:T(8,128)S(1)} %get-tuple-element.7.diag_ref, f32[20,16,128]{2,1,0:T(8,128)S(1)} %get-tuple-element.6.right_ref), custom_call_target="tpu_custom_call" | custom-call | tf_op jit(solution)/shard_map/conjugate_gradients/pallas_call | solution.py:316
  244.3 0.1 copy.10
  244.4 0.8 reshape.91
  245.2 0.1 copy.11
  245.3 0.8 reshape.92
  (2 shorter events, 0.0 us)
Async XLA Ops:
  10.1 10.4 %copy-start.1 = (f32[16,40]{1,0:T(8,128)S(1)}, f32[16,40]{1,0:T(8,128)}, u32[]{:S(2)}) copy-start(f32[16,40]{1,0:T(8,128)} %param.5) | copy-start | bytes 7684
  10.1 10.6 %copy-start = (f32[16,40,64]{2,1,0:T(8,128)S(1)}, f32[16,40,64]{2,1,0:T(8,128)}, u32[]{:S(2)}) copy-start(f32[16,40,64]{2,1,0:T(8,128)} %param.6) | copy-start | bytes 491524

commit v2 on v0

v2 whole, which is shorter than its diff:
```python
import functools

import jax
import jax.numpy as jnp
from jax import lax
from jax.experimental import pallas as pl
from jax.experimental.pallas import tpu as pltpu
from jax.sharding import PartitionSpec as P

ITERS = 3
NX = 4
CHUNKS = 4
ROWS = 32
MESH = pl.DeviceIdType.MESH
F32 = jnp.float32
BF16 = jnp.bfloat16
LANES = 128
HALF = 64
CELLS = 16


def column_sums(values):
    total = jnp.sum(jnp.sum(values, axis=0), axis=0, keepdims=True)
    return total + pltpu.roll(total, HALF, 1)


def kernel(
    nx, nz,
    first_ref, matrix_hbm, diag_ref, right_ref,
    sol_ref, res_ref,
    raw, matrix, gathered, mirror, got_x, sums_z, got_z,
    direction, image, slab_dir, slab_img,
    out1, in1, out2, in2, out_a, in_a, out_b, in_b, out_s, in_s,
    load_sem, gz_send, gz_recv, gx_send, gx_recv,
    mx_send, mx_recv, mz_send, mz_recv, hop_send, hop_recv,
):
    n = nx * nz
    pairs = diag_ref.shape[0]
    order = n * CELLS
    block_rows, _, blocks, _ = raw.shape
    per_chunk = pairs // CHUNKS
    turn_rows = min(ROWS, order)
    i = lax.axis_index("row")
    j = lax.axis_index("col")
    z = i // nx
    x = i % nx
    first = first_ref[0]
    my_row = (j - first) & (n - 1)
    my_block = (first + my_row) // n
    my_col = (first + i) & (n - 1)
    odd = (my_block & 1) == 1

    def load(a):
        return pltpu.make_async_copy(matrix_hbm.at[a], raw.at[a], load_sem.at[a])

    for a in range(block_rows):
        load(a).start()

    block_of = (
        2 * lax.broadcasted_iota(jnp.int32, (pairs, CELLS, LANES), 0)
        + lax.broadcasted_iota(jnp.int32, (pairs, CELLS, LANES), 2) // HALF
    )
    owned = (block_of == my_block) | (block_of == my_block + 1)
    slot_of = lax.broadcasted_iota(jnp.int32, (n, CELLS, LANES), 0)
    left_half = lax.broadcasted_iota(jnp.int32, (order, LANES), 1) < HALF
    even_lanes = (lax.broadcasted_iota(jnp.int32, (CELLS, LANES), 1) < HALF).astype(F32)
    even_mask = even_lanes.astype(BF16)
    odd_mask = (1.0 - even_lanes).astype(BF16)

    def swap(piece):
        return jnp.where(odd, pltpu.roll(piece, HALF, 1), piece)

    def chosen(slots, which):
        return jnp.sum(jnp.where(slot_of == which, slots.astype(F32), 0.0), axis=0)

    def row_copy(src, dst, send, recv, zz, xx):
        return pltpu.make_async_remote_copy(
            src_ref=src, dst_ref=dst, send_sem=send, recv_sem=recv,
            device_id=(zz * nx + xx, j), device_id_type=MESH,
        )

    def hop_copy(src, dst, k, h, row, col):
        return pltpu.make_async_remote_copy(
            src_ref=src, dst_ref=dst, send_sem=hop_send.at[k, h],
            recv_sem=hop_recv.at[k, h], device_id=(row, col), device_id_type=MESH,
        )

    def hop_wait(buf, k, h, slots):
        part = buf.at[pl.ds(0, slots)]
        hop_copy(part, part, k, h, i, j).wait()

    def cross_start(src, dst, k, h, target):
        def send(step, c):
            row, col = target(step)

            @pl.when((row != i) | (col != j))
            def _():
                hop_copy(src, dst, k, h, row, col).start()

            return c

        lax.fori_loop(0, n, send, 0)

    def cross_wait(buf, k, h):
        @pl.when(i == j)
        def _():
            hop_wait(buf, k, h, n - 1)

        @pl.when(i != j)
        def _():
            hop_wait(buf, k, h, n)

    def line_start(src, dst, k, h, target):
        def send(step, c):
            row, col = target(step)
            hop_copy(src(row, col), dst, k, h, row, col).start()
            return c

        lax.fori_loop(1, n, send, 0)

    def along_col(step):
        return i, (j + step) % n

    def along_row(step):
        return (i + step) % n, j

    def sums_col(k, h, value):
        out_s[k, h] = value
        in_s[k, h, j] = value
        line_start(lambda r, c: out_s.at[k, h], in_s.at[k, h, j], k, 4 + h, along_col)

    def sums_row(k, h):
        hop_wait(in_s.at[k, h], k, 4 + h, n - 1)
        value = jnp.sum(in_s[k, h], axis=0)
        out_s[k, h + 1] = value
        in_s[k, h + 1, i] = value
        line_start(lambda r, c: out_s.at[k, h + 1], in_s.at[k, h + 1, i], k, 5 + h, along_row)

    def sums_end(k, h):
        hop_wait(in_s.at[k, h + 1], k, 5 + h, n - 1)
        return jnp.sum(in_s[k, h + 1], axis=0)

    def spread_z(k, dz):
        return row_copy(
            gathered.at[k, z, x], gathered.at[k, z, x],
            gz_send.at[k, dz - 1], gz_recv.at[k, dz - 1], (z + dz) % nz, x,
        )

    def spread_x(k, dx, dz):
        zz = (z - dz + nz) % nz
        return row_copy(
            gathered.at[k, zz, x], gathered.at[k, zz, x],
            gx_send.at[k, dz, dx - 1], gx_recv.at[k, dz, dx - 1], z, (x + dx) % nx,
        )

    def forward_z(k, dz):
        spread_z(k, dz).wait()
        for dx in range(1, nx):
            spread_x(k, dx, dz).start()

    def start(k, residual):
        out1[k] = swap(jnp.sum(jnp.where(owned, residual, 0.0), axis=0)).astype(BF16)

        @pl.when(i == j)
        def _():
            in1[k, j] = out1[k]

        cross_start(out1.at[k], in1.at[k, j], k, 0, lambda step: ((i + step) % n, i))
        gathered[k, z, x] = residual.astype(BF16)
        for dz in range(1, nz):
            spread_z(k, dz).start()
        for dx in range(1, nx):
            spread_x(k, dx, 0).start()
        sums_col(k, 0, column_sums(residual * residual))

    sol_ref[...] = jnp.zeros_like(sol_ref)
    res_ref[...] = right_ref[...]
    direction[...] = jnp.zeros_like(direction)
    image[...] = jnp.zeros_like(image)
    slab_dir[...] = jnp.zeros_like(slab_dir)
    slab_img[...] = jnp.zeros_like(slab_img)
    start(0, right_ref[...])

    for a in range(block_rows):
        load(a).wait()
        slab_row = first + a * n + i

        def turn(q, c, a=a, slab_row=slab_row):
            at = pl.ds(pl.multiple_of(q * turn_rows, turn_rows), turn_rows)
            to = pl.ds(pl.multiple_of(a * order + q * turn_rows, turn_rows), turn_rows)
            for tile in range(blocks // 8):
                values = jnp.swapaxes(raw[a, at, tile * 8 : tile * 8 + 8, :], 0, 1)
                for b in range(8):
                    column = (tile * 8 + b) * n + j
                    weight = jnp.where(
                        column < slab_row, 1.0, jnp.where(column == slab_row, 0.5, 0.0)
                    )
                    matrix[tile * 8 + b, to] = values[b] * weight.astype(BF16)
            return c

        lax.fori_loop(0, order // turn_rows, turn, 0)

    def iteration(k, norm_old):
        residual = res_ref[...]
        cross_wait(in1.at[k], k, 0)
        out2[k] = chosen(in1[k], my_col).astype(BF16)
        in2[k, j] = out2[k]
        line_start(lambda r, c: out2.at[k], in2.at[k, j], k, 1, along_col)
        sums_row(k, 0)
        for dz in range(1, nz):
            forward_z(k, dz)
        hop_wait(in2.at[k], k, 1, n - 1)
        slab = in2[k].astype(F32).reshape(order, LANES)

        turned = jnp.transpose(slab).astype(BF16)
        both = jnp.concatenate([turned[0:HALF], turned[HALF:LANES]], axis=1)

        def mirror_x(chunk, dx):
            xx = (x + dx) % nx
            return row_copy(
                mirror.at[chunk, :, xx], got_x.at[k, chunk, dx - 1],
                mx_send.at[k, chunk, dx - 1], mx_recv.at[k, chunk, dx - 1], z, xx,
            )

        def mirror_z(chunk, dz):
            zz = (z + dz) % nz
            return row_copy(
                sums_z.at[chunk, zz], got_z.at[k, chunk, dz - 1],
                mz_send.at[k, chunk, dz - 1], mz_recv.at[k, chunk, dz - 1], zz, x,
            )

        def transposed(chunk, c):
            for u in range(per_chunk):
                p = chunk * per_chunk + u
                parts = [
                    jnp.dot(both, matrix[2 * p + h], preferred_element_type=F32)
                    for h in range(2)
                ]
                cells = jnp.transpose(jnp.concatenate(parts, axis=0))
                mirror[chunk, :, :, u] = cells.astype(BF16).reshape(nz, nx, CELLS, LANES)
            for dx in range(1, nx):
                mirror_x(chunk, dx).start()
            return c

        lax.fori_loop(0, CHUNKS, transposed, 0)

        norm = sums_end(k, 0)
        beta = jnp.where(k == 0, 0.0, norm / norm_old)
        slab_d = slab + beta * slab_dir[...]
        slab_dir[...] = slab_d
        beta_cell = beta.reshape(1, 1, LANES)
        cells_d = residual + beta_cell * direction[...]
        direction[...] = cells_d
        curve = column_sums(diag_ref[...] * cells_d * cells_d)

        for dz in range(nz):
            for dx in range(1, nx):
                spread_x(k, dx, dz).wait()
        rows = None
        for half in range(2):
            left, right = [], []
            for u in range(pairs // 2):
                p = half * (pairs // 2) + u
                cells = gathered[k, :, :, p].reshape(n, CELLS, LANES)
                left += [matrix[2 * p], matrix[2 * p + 1]]
                right += [
                    (cells * even_mask).reshape(order, LANES),
                    (cells * odd_mask).reshape(order, LANES),
                ]
            part = jnp.dot(
                jnp.concatenate(left, axis=1),
                jnp.concatenate(right, axis=0),
                preferred_element_type=F32,
            )
            rows = part if rows is None else rows + part
        rows = rows + pltpu.roll(rows, HALF, 1)
        rows = jnp.where(left_half, rows[0:order], rows[order:])

        out_a[k] = rows.astype(BF16).reshape(n, CELLS, LANES)
        in_a[k, j] = out_a[k, j]
        line_start(lambda r, c: out_a.at[k, c], in_a.at[k, j], k, 2, along_col)
        slab_q = rows + beta * slab_img[...]
        slab_img[...] = slab_q
        curve = curve + 2.0 * column_sums((slab_d * slab_q).reshape(n, CELLS, LANES))
        sums_col(k, 2, curve)

        def pass_z(chunk, c):
            for dx in range(1, nx):
                mirror_x(chunk, dx).wait()
            for dz in range(nz):
                zz = (z + dz) % nz
                total = mirror[chunk, zz, x].astype(F32)
                for dx in range(1, nx):
                    total = total + got_x[k, chunk, dx - 1, zz].astype(F32)
                sums_z[chunk, zz] = total.astype(BF16)
            for dz in range(1, nz):
                mirror_z(chunk, dz).start()
            return c

        lax.fori_loop(0, CHUNKS // 2, pass_z, 0)

        hop_wait(in_a.at[k], k, 2, n - 1)
        out_b[k] = jnp.sum(in_a[k].astype(F32), axis=0).astype(BF16)

        @pl.when(i == j)
        def _():
            in_b[k, i] = out_b[k]

        cross_start(out_b.at[k], in_b.at[k, i], k, 3, lambda step: (j, (j + step) % n))
        sums_row(k, 2)
        lax.fori_loop(CHUNKS // 2, CHUNKS, pass_z, 0)

        def finish_z(chunk, c):
            for dz in range(1, nz):
                mirror_z(chunk, dz).wait()
            at = pl.ds(chunk * per_chunk, per_chunk)
            total = sums_z[chunk, z].astype(F32)
            for dz in range(1, nz):
                total = total + got_z[k, chunk, dz - 1].astype(F32)
            image[at] = beta_cell * image[at] + total
            return c

        lax.fori_loop(0, CHUNKS, finish_z, 0)
        applied = image[...] + diag_ref[...] * residual

        cross_wait(in_b.at[k], k, 3)
        piece = swap(chosen(in_b[k], my_row))
        applied = applied + jnp.where(owned, piece.reshape(1, CELLS, LANES), 0.0)
        image[...] = applied
        length = (norm / sums_end(k, 2)).reshape(1, 1, LANES)
        sol_ref[...] = sol_ref[...] + length * cells_d
        residual = residual - length * applied
        res_ref[...] = residual

        @pl.when(k < ITERS - 1)
        def _():
            start(k + 1, residual)

        return norm

    lax.fori_loop(0, ITERS, iteration, jnp.ones((1, LANES), F32))


def body(nx, matrix, diagonal, right_side, slab_first):
    n = lax.axis_size("row")
    nz = n // nx
    rb, order, blocks, _ = matrix.shape
    cells, _, width = right_side.shape
    pairs = blocks // 2
    per_chunk = pairs // CHUNKS

    def packed(cell_array):
        return jnp.transpose(cell_array.reshape(cells, pairs, LANES), (1, 0, 2))

    def unpacked(cell_array):
        return jnp.transpose(cell_array, (1, 0, 2)).reshape(cells, blocks, width)

    diag = packed(jnp.broadcast_to(diagonal[:, :, None], right_side.shape))
    vec = (pairs, cells, LANES)
    part = (per_chunk, cells, LANES)
    piece = (cells, LANES)
    vmem = pl.BlockSpec(memory_space=pltpu.VMEM)
    dma = pltpu.SemaphoreType.DMA
    sol, res = pl.pallas_call(
        functools.partial(kernel, nx, nz),
        out_shape=[jax.ShapeDtypeStruct(vec, F32)] * 2,
        in_specs=[
            pl.BlockSpec(memory_space=pltpu.SMEM),
            pl.BlockSpec(memory_space=pl.ANY),
            vmem,
            vmem,
        ],
        out_specs=[vmem, vmem],
        scratch_shapes=[
            pltpu.VMEM(matrix.shape, BF16),
            pltpu.VMEM((blocks, rb * order, order), BF16),
            pltpu.VMEM((ITERS, nz, nx) + vec, BF16),
            pltpu.VMEM((CHUNKS, nz, nx) + part, BF16),
            pltpu.VMEM((ITERS, CHUNKS, nx - 1, nz) + part, BF16),
            pltpu.VMEM((CHUNKS, nz) + part, BF16),
            pltpu.VMEM((ITERS, CHUNKS, nz - 1) + part, BF16),
            pltpu.VMEM(vec, F32),
            pltpu.VMEM(vec, F32),
            pltpu.VMEM((order, LANES), F32),
            pltpu.VMEM((order, LANES), F32),
            pltpu.VMEM((ITERS,) + piece, BF16),
            pltpu.VMEM((ITERS, n) + piece, BF16),
            pltpu.VMEM((ITERS,) + piece, BF16),
            pltpu.VMEM((ITERS, n) + piece, BF16),
            pltpu.VMEM((ITERS, n) + piece, BF16),
            pltpu.VMEM((ITERS, n) + piece, BF16),
            pltpu.VMEM((ITERS,) + piece, BF16),
            pltpu.VMEM((ITERS, n) + piece, BF16),
            pltpu.VMEM((ITERS, 4, 1, LANES), F32),
            pltpu.VMEM((ITERS, 4, n, 1, LANES), F32),
            dma((rb,)),
            dma((ITERS, nz - 1)),
            dma((ITERS, nz - 1)),
            dma((ITERS, nz, nx - 1)),
            dma((ITERS, nz, nx - 1)),
            dma((ITERS, CHUNKS, nx - 1)),
            dma((ITERS, CHUNKS, nx - 1)),
            dma((ITERS, CHUNKS, nz - 1)),
            dma((ITERS, CHUNKS, nz - 1)),
            dma((ITERS, 8)),
            dma((ITERS, 8)),
        ],
        compiler_params=pltpu.CompilerParams(
            has_side_effects=True, vmem_limit_bytes=56 * 1024 * 1024
        ),
        name="conjugate_gradients",
    )(slab_first, matrix, diag, packed(right_side))
    return unpacked(sol), unpacked(res)


def solution(mesh, nx=NX):
    placed = (
        P(None, "row", None, "col"),
        P(("col", "row"), None),
        P(("col", "row"), None, None),
        P(),
    )
    return jax.shard_map(
        functools.partial(body, nx),
        mesh=mesh,
        in_specs=placed,
        out_specs=(P(("col", "row"), None, None), P(("col", "row"), None, None)),
        check_vma=False,
    )
```

time: 1650 us -> 167 us (0.10)
  waiting for transfers between devices: 1130 us -> 0 us
  blocking collectives: 373 us -> 0 us
  Pallas kernels: 0 us -> 159 us
  matrix products: 66.4 us -> 0 us
  local copies, waits for them, and re-layouts: 60 us -> 6.42 us
    psum x6 -> x0, waiting for transfers between devices: 649 us -> none  [the longest x3 357 us: body(): row_total_sum = lax.psum(row_part, 'col')]
    psum x5 -> x0, blocking collectives: 373 us -> none  [the longest x3 221 us: squares(): return lax.psum(jnp.sum(residual * residual, axis=(0, 1)), ('row', 'col'))]
    reduce_scatter x3 -> x0, waiting for transfers between devices: 301 us -> none  [body(): offdiag = lax.psum_scatter(total, 'row', scatter_dimension=0, tiled=True)]
    all_gather x3 -> x0, waiting for transfers between devices: 175 us -> none  [body(): lax.all_gather(vector.astype(jnp.bfloat16), 'row', axis=0, tiled=True)]
    pallas_call x0 -> x1, Pallas kernels: none -> 159 us  [body(): pl.pallas_call(functools.partial(kernel, nx, nz), out_shape=[jax.ShapeDty...]
    dot_general x15 -> x0, matrix products: 66.4 us -> none  [the longest x6 26.8 us: body(): jnp.einsum('vjx,vo->xjo', matrix[index_position], slab_direction[index_po...]
    all_gather x6 -> x0, local copies, waits for them, and re-layouts: 28.3 us -> none  [body(): lax.all_gather(vector.astype(jnp.bfloat16), 'row', axis=0, tiled=True)]
    add x3 -> x0, local copies, waits for them, and re-layouts: 18.1 us -> none  [body(): offdiag + lax.psum_scatter(positioned_rows, 'row', scatter_dimension=0, t...]
  transfers between devices with their start and end apart: 12 -> 0, of which waited for: 12 -> 0; matrix products, arithmetic and copies ran while one was open for 3% -> 0% of each run, Pallas kernels for 0% -> 0%
where the time goes in v2:
time: 167 us
  Pallas kernels  159 us (95%)
  local copies, waits for them, and re-layouts  6.42 us (4%)
    pallas_call x1, Pallas kernels, body(): pl.pallas_call(functools.partial(kernel, nx, nz), out_shape=[jax.ShapeDty...  159 us

profile of v2, /device:TPU:1, one launch (start us, length us, event | category | flops | bytes accessed | tf_op | source)
XLA Modules:
  0.0 166.7 jit_solution(9055718074807534460)
XLA Ops:
  1.3 1.1 reshape.18
  2.4 0.8 broadcast_in_dim.2
  3.2 0.1 reshape.17
  3.3 0.8 copy_bitcast_fusion
  4.1 159.0 %conjugate_gradients.1 = (f32[20,16,128]{2,1,0:T(8,128)}, f32[20,16,128]{2,1,0:T(8,128)}) custom-call(s32[1]{0:T(128)S(6)} %copy.12.first_ref, bf16[2,256,40,256]{3,2,1,0:T(8,128)(2,1)} %matrix_hbm.1, f32[20,16,128]{2,1,0:T(8,128)} %get-tuple-element.7.diag_ref, f32[20,16,128]{2,1,0:T(8,128)} %get-tuple-element.6.right_ref), custom_call_target="tpu_custom_call" | custom-call | tf_op jit(solution)/shard_map/conjugate_gradients/pallas_call | solution.py:364
  163.1 1.0 copy.9
  164.1 1.0 copy.8
  165.1 0.8 reshape.19
  165.9 0.8 reshape.20

commit v3 on v2

--- a/solution.py
+++ b/solution.py
@@ -25,20 +25,21 @@
 
 
 def kernel(
-    nx, nz,
+    nx, nz, live,
     first_ref, matrix_hbm, diag_ref, right_ref,
     sol_ref, res_ref,
     raw, matrix, gathered, mirror, got_x, sums_z, got_z,
-    direction, image, slab_dir, slab_img,
+    diagonal, direction, image, solution, residual_ref, slab_dir, slab_img,
     out1, in1, out2, in2, out_a, in_a, out_b, in_b, out_s, in_s,
     load_sem, gz_send, gz_recv, gx_send, gx_recv,
     mx_send, mx_recv, mz_send, mz_recv, hop_send, hop_recv,
 ):
     n = nx * nz
-    pairs = diag_ref.shape[0]
+    pairs = diagonal.shape[0]
     order = n * CELLS
-    block_rows, _, blocks, _ = raw.shape
-    per_chunk = pairs // CHUNKS
+    block_rows = raw.shape[0]
+    stored = raw.shape[2]
+    per_chunk = live // CHUNKS
     turn_rows = min(ROWS, order)
     i = lax.axis_index("row")
     j = lax.axis_index("col")
@@ -51,7 +52,9 @@
     odd = (my_block & 1) == 1
 
     def load(a):
-        return pltpu.make_async_copy(matrix_hbm.at[a], raw.at[a], load_sem.at[a])
+        return pltpu.make_async_copy(
+            matrix_hbm.at[a, :, pl.ds(0, stored)], raw.at[a], load_sem.at[a]
+        )
 
     for a in range(block_rows):
         load(a).start()
@@ -165,21 +168,32 @@
         def _():
             in1[k, j] = out1[k]
 
-        cross_start(out1.at[k], in1.at[k, j], k, 0, lambda step: ((i + step) % n, i))
-        gathered[k, z, x] = residual.astype(BF16)
+        cross_start(out1.at[k], in1.at[k, j], k, 0, lambda step: ((j + step) % n, i))
+        gathered[k, z, x] = residual[0:live].astype(BF16)
         for dz in range(1, nz):
             spread_z(k, dz).start()
         for dx in range(1, nx):
             spread_x(k, dx, 0).start()
         sums_col(k, 0, column_sums(residual * residual))
 
-    sol_ref[...] = jnp.zeros_like(sol_ref)
-    res_ref[...] = right_ref[...]
+    for tile in range(2 * pairs // 8):
+        values = jnp.swapaxes(right_ref[:, tile * 8 : tile * 8 + 8, :], 0, 1)
+        for u in range(4):
+            at = tile * 4 + u
+            residual_ref[at] = jnp.concatenate([values[2 * u], values[2 * u + 1]], axis=1)
+            diagonal[at] = jnp.concatenate(
+                [
+                    jnp.broadcast_to(diag_ref[:, 2 * at + h : 2 * at + h + 1], (CELLS, HALF))
+                    for h in range(2)
+                ],
+                axis=1,
+            )
+    solution[...] = jnp.zeros_like(solution)
     direction[...] = jnp.zeros_like(direction)
     image[...] = jnp.zeros_like(image)
     slab_dir[...] = jnp.zeros_like(slab_dir)
     slab_img[...] = jnp.zeros_like(slab_img)
-    start(0, right_ref[...])
+    start(0, residual_ref[...])
 
     for a in range(block_rows):
         load(a).wait()
@@ -188,7 +202,7 @@
         def turn(q, c, a=a, slab_row=slab_row):
             at = pl.ds(pl.multiple_of(q * turn_rows, turn_rows), turn_rows)
             to = pl.ds(pl.multiple_of(a * order + q * turn_rows, turn_rows), turn_rows)
-            for tile in range(blocks // 8):
+            for tile in range(live // 4):
                 values = jnp.swapaxes(raw[a, at, tile * 8 : tile * 8 + 8, :], 0, 1)
                 for b in range(8):
                     column = (tile * 8 + b) * n + j
@@ -201,14 +215,17 @@
         lax.fori_loop(0, order // turn_rows, turn, 0)
 
     def iteration(k, norm_old):
-        residual = res_ref[...]
+        residual = residual_ref[...]
+        forward_z(k, 1)
+        if nz > 2:
+            forward_z(k, nz - 1)
         cross_wait(in1.at[k], k, 0)
         out2[k] = chosen(in1[k], my_col).astype(BF16)
         in2[k, j] = out2[k]
         line_start(lambda r, c: out2.at[k], in2.at[k, j], k, 1, along_col)
+        for dz in range(2, nz - 1):
+            forward_z(k, dz)
         sums_row(k, 0)
-        for dz in range(1, nz):
-            forward_z(k, dz)
         hop_wait(in2.at[k], k, 1, n - 1)
         slab = in2[k].astype(F32).reshape(order, LANES)
 
@@ -251,7 +268,7 @@
         beta_cell = beta.reshape(1, 1, LANES)
         cells_d = residual + beta_cell * direction[...]
         direction[...] = cells_d
-        curve = column_sums(diag_ref[...] * cells_d * cells_d)
+        curve = column_sums(diagonal[...] * cells_d * cells_d)
 
         for dz in range(nz):
             for dx in range(1, nx):
@@ -259,8 +276,8 @@
         rows = None
         for half in range(2):
             left, right = [], []
-            for u in range(pairs // 2):
-                p = half * (pairs // 2) + u
+            for u in range(live // 2):
+                p = half * (live // 2) + u
                 cells = gathered[k, :, :, p].reshape(n, CELLS, LANES)
                 left += [matrix[2 * p], matrix[2 * p + 1]]
                 right += [
@@ -306,7 +323,7 @@
         def _():
             in_b[k, i] = out_b[k]
 
-        cross_start(out_b.at[k], in_b.at[k, i], k, 3, lambda step: (j, (j + step) % n))
+        cross_start(out_b.at[k], in_b.at[k, i], k, 3, lambda step: (j, (i + step) % n))
         sums_row(k, 2)
         lax.fori_loop(CHUNKS // 2, CHUNKS, pass_z, 0)
 
@@ -317,20 +334,21 @@
             total = sums_z[chunk, z].astype(F32)
             for dz in range(1, nz):
                 total = total + got_z[k, chunk, dz - 1].astype(F32)
-            image[at] = beta_cell * image[at] + total
-            return c
-
+            image[at] = image[at] + total
+            return c
+
+        image[...] = beta_cell * image[...] + diagonal[...] * residual
         lax.fori_loop(0, CHUNKS, finish_z, 0)
-        applied = image[...] + diag_ref[...] * residual
+        applied = image[...]
 
         cross_wait(in_b.at[k], k, 3)
         piece = swap(chosen(in_b[k], my_row))
         applied = applied + jnp.where(owned, piece.reshape(1, CELLS, LANES), 0.0)
         image[...] = applied
         length = (norm / sums_end(k, 2)).reshape(1, 1, LANES)
-        sol_ref[...] = sol_ref[...] + length * cells_d
+        solution[...] = solution[...] + length * cells_d
         residual = residual - length * applied
-        res_ref[...] = residual
+        residual_ref[...] = residual
 
         @pl.when(k < ITERS - 1)
         def _():
@@ -339,78 +357,87 @@
         return norm
 
     lax.fori_loop(0, ITERS, iteration, jnp.ones((1, LANES), F32))
+    for source, target in ((solution, sol_ref), (residual_ref, res_ref)):
+        for tile in range(2 * pairs // 8):
+            halves = []
+            for u in range(4):
+                values = source[tile * 4 + u]
+                halves += [values[:, 0:HALF], values[:, HALF:LANES]]
+            target[:, tile * 8 : tile * 8 + 8, :] = jnp.swapaxes(jnp.stack(halves), 0, 1)
 
 
 def body(nx, matrix, diagonal, right_side, slab_first):
     n = lax.axis_size("row")
     nz = n // nx
     rb, order, blocks, _ = matrix.shape
-    cells, _, width = right_side.shape
+    cells = right_side.shape[0]
     pairs = blocks // 2
-    per_chunk = pairs // CHUNKS
-
-    def packed(cell_array):
-        return jnp.transpose(cell_array.reshape(cells, pairs, LANES), (1, 0, 2))
-
-    def unpacked(cell_array):
-        return jnp.transpose(cell_array, (1, 0, 2)).reshape(cells, blocks, width)
-
-    diag = packed(jnp.broadcast_to(diagonal[:, :, None], right_side.shape))
     vec = (pairs, cells, LANES)
-    part = (per_chunk, cells, LANES)
     piece = (cells, LANES)
     vmem = pl.BlockSpec(memory_space=pltpu.VMEM)
     dma = pltpu.SemaphoreType.DMA
-    sol, res = pl.pallas_call(
-        functools.partial(kernel, nx, nz),
-        out_shape=[jax.ShapeDtypeStruct(vec, F32)] * 2,
-        in_specs=[
-            pl.BlockSpec(memory_space=pltpu.SMEM),
-            pl.BlockSpec(memory_space=pl.ANY),
-            vmem,
-            vmem,
-        ],
-        out_specs=[vmem, vmem],
-        scratch_shapes=[
-            pltpu.VMEM(matrix.shape, BF16),
-            pltpu.VMEM((blocks, rb * order, order), BF16),
-            pltpu.VMEM((ITERS, nz, nx) + vec, BF16),
-            pltpu.VMEM((CHUNKS, nz, nx) + part, BF16),
-            pltpu.VMEM((ITERS, CHUNKS, nx - 1, nz) + part, BF16),
-            pltpu.VMEM((CHUNKS, nz) + part, BF16),
-            pltpu.VMEM((ITERS, CHUNKS, nz - 1) + part, BF16),
-            pltpu.VMEM(vec, F32),
-            pltpu.VMEM(vec, F32),
-            pltpu.VMEM((order, LANES), F32),
-            pltpu.VMEM((order, LANES), F32),
-            pltpu.VMEM((ITERS,) + piece, BF16),
-            pltpu.VMEM((ITERS, n) + piece, BF16),
-            pltpu.VMEM((ITERS,) + piece, BF16),
-            pltpu.VMEM((ITERS, n) + piece, BF16),
-            pltpu.VMEM((ITERS, n) + piece, BF16),
-            pltpu.VMEM((ITERS, n) + piece, BF16),
-            pltpu.VMEM((ITERS,) + piece, BF16),
-            pltpu.VMEM((ITERS, n) + piece, BF16),
-            pltpu.VMEM((ITERS, 4, 1, LANES), F32),
-            pltpu.VMEM((ITERS, 4, n, 1, LANES), F32),
-            dma((rb,)),
-            dma((ITERS, nz - 1)),
-            dma((ITERS, nz - 1)),
-            dma((ITERS, nz, nx - 1)),
-            dma((ITERS, nz, nx - 1)),
-            dma((ITERS, CHUNKS, nx - 1)),
-            dma((ITERS, CHUNKS, nx - 1)),
-            dma((ITERS, CHUNKS, nz - 1)),
-            dma((ITERS, CHUNKS, nz - 1)),
-            dma((ITERS, 8)),
-            dma((ITERS, 8)),
-        ],
-        compiler_params=pltpu.CompilerParams(
-            has_side_effects=True, vmem_limit_bytes=56 * 1024 * 1024
-        ),
-        name="conjugate_gradients",
-    )(slab_first, matrix, diag, packed(right_side))
-    return unpacked(sol), unpacked(res)
+
+    def solve(live):
+        stored = min(blocks, -(-2 * live // 16) * 16)
+        shard = (live, cells, LANES)
+        part = (live // CHUNKS, cells, LANES)
+        return pl.pallas_call(
+            functools.partial(kernel, nx, nz, live),
+            out_shape=[jax.ShapeDtypeStruct(right_side.shape, F32)] * 2,
+            in_specs=[
+                pl.BlockSpec(memory_space=pltpu.SMEM),
+                pl.BlockSpec(memory_space=pl.ANY),
+                vmem,
+                vmem,
+            ],
+            out_specs=[vmem, vmem],
+            scratch_shapes=[
+                pltpu.VMEM((rb, order, stored, order), BF16),
+                pltpu.VMEM((2 * live, rb * order, order), BF16),
+                pltpu.VMEM((ITERS, nz, nx) + shard, BF16),
+                pltpu.VMEM((CHUNKS, nz, nx) + part, BF16),
+                pltpu.VMEM((ITERS, CHUNKS, nx - 1, nz) + part, BF16),
+                pltpu.VMEM((CHUNKS, nz) + part, BF16),
+                pltpu.VMEM((ITERS, CHUNKS, nz - 1) + part, BF16),
+                pltpu.VMEM(vec, F32),
+                pltpu.VMEM(vec, F32),
+                pltpu.VMEM(vec, F32),
+                pltpu.VMEM(vec, F32),
+                pltpu.VMEM(vec, F32),
+                pltpu.VMEM((order, LANES), F32),
+                pltpu.VMEM((order, LANES), F32),
+                pltpu.VMEM((ITERS,) + piece, BF16),
+                pltpu.VMEM((ITERS, n) + piece, BF16),
+                pltpu.VMEM((ITERS,) + piece, BF16),
+                pltpu.VMEM((ITERS, n) + piece, BF16),
+                pltpu.VMEM((ITERS, n) + piece, BF16),
+                pltpu.VMEM((ITERS, n) + piece, BF16),
+                pltpu.VMEM((ITERS,) + piece, BF16),
+                pltpu.VMEM((ITERS, n) + piece, BF16),
+                pltpu.VMEM((ITERS, 4, 1, LANES), F32),
+                pltpu.VMEM((ITERS, 4, n, 1, LANES), F32),
+                dma((rb,)),
+                dma((ITERS, nz - 1)),
+                dma((ITERS, nz - 1)),
+                dma((ITERS, nz, nx - 1)),
+                dma((ITERS, nz, nx - 1)),
+                dma((ITERS, CHUNKS, nx - 1)),
+                dma((ITERS, CHUNKS, nx - 1)),
+                dma((ITERS, CHUNKS, nz - 1)),
+                dma((ITERS, CHUNKS, nz - 1)),
+                dma((ITERS, 8)),
+                dma((ITERS, 8)),
+            ],
+            compiler_params=pltpu.CompilerParams(
+                has_side_effects=True, vmem_limit_bytes=56 * 1024 * 1024
+            ),
+            name=f"conjugate_gradients_{live}",
+        )(slab_first, matrix, diagonal, right_side)
+
+    lives = range(CHUNKS, pairs + 1, CHUNKS)
+    used = (slab_first[0] + rb * n - 1) // n + 1
+    branch = jnp.clip((used + 2 * CHUNKS - 1) // (2 * CHUNKS) - 1, 0, len(lives) - 1)
+    return lax.switch(branch, [functools.partial(solve, live) for live in lives])
 
 
 def solution(mesh, nx=NX):

time: 167 us -> 112 us (0.67)
  Pallas kernels: 159 us -> 109 us
  local copies, waits for them, and re-layouts: 6.42 us -> 1.45 us
    pallas_call x1, Pallas kernels: 159 us -> 109 us  [solve(): pl.pallas_call(functools.partial(kernel, nx, nz, live), out_shape=[jax.Sh...]
    reshape x4 -> x0, local copies, waits for them, and re-layouts: 2.85 us -> none  [the longest x2 1.67 us: unpacked(): return jnp.transpose(cell_array, (1, 0, 2)).reshape(cells, blocks, width)]
    transpose x3 -> x0, local copies, waits for them, and re-layouts: 2.73 us -> none  [the longest x2 1.94 us: unpacked(): return jnp.transpose(cell_array, (1, 0, 2)).reshape(cells, blocks, width)]
where the time goes in v3:
time: 112 us
  Pallas kernels  109 us (97%)
  local copies, waits for them, and re-layouts  1.45 us (1%)
  between operations  1.33 us (1%)
    pallas_call x1, Pallas kernels, solve(): pl.pallas_call(functools.partial(kernel, nx, nz, live), out_shape=[jax.Sh...  109 us

profile of v3, /device:TPU:1, one launch (start us, length us, event | category | flops | bytes accessed | tf_op | source)
XLA Modules:
  0.0 112.2 jit_solution(9086179228298463653)
XLA Ops:
  1.3 109.4 %conditional.1 = ((f32[16,40,64]{2,1,0:T(8,128)S(1)}, f32[16,40,64]{2,1,0:T(8,128)S(1)})) conditional(s32[]{:T(128)} %clamp.3, (s32[1]{0:T(128)}, bf16[2,256,40,256]{3,2,1,0:T(8,128)(2,1)}, f32[16,40]{1,0:T(8,128)}, f32[16,40,64]{2,1,0:T(8,128)}) %tuple.22, (s32[1]{0:T(128)}, bf16[2,256,40,256]{3,2,1,0:T(8,128)(2,1)}, ...), branch_computations={%region_0.1_spmd, %region_1.2_spmd, %region_2.3_spmd, %region_3.4_... | conditional | bytes 8 | solution.py:440
  1.3 109.2 %conjugate_gradients_4.1 = (f32[16,40,64]{2,1,0:T(8,128)S(1)}, f32[16,40,64]{2,1,0:T(8,128)S(1)}) custom-call(s32[1]{0:T(128)} %get-tuple-element.40.first_ref, bf16[2,256,40,256]{3,2,1,0:T(8,128)(2,1)} %get-tuple-element.89.matrix_hbm, f32[16,40]{1,0:T(8,128)} %get-tuple-element.94.diag_ref, f32[16,40,64]{2,1,0:T(8,128)} %get-tuple-element.99.right_ref), custom_call_target="tpu_custom_call" | custom-call | tf_op jit(solution)/shard_map/cond/branch_0_fun/conjugate_gradients_4/pallas_call | solution.py:384
  110.8 0.7 copy.44
  111.5 0.7 copy.45

commit v4 on v3

--- a/solution.py
+++ b/solution.py
@@ -28,11 +28,11 @@
     nx, nz, live,
     first_ref, matrix_hbm, diag_ref, right_ref,
     sol_ref, res_ref,
-    raw, matrix, gathered, mirror, got_x, sums_z, got_z,
+    raw, matrix, gathered, mirror, got_x, sums_z, got_z, first_z, sums_x, last_x,
     diagonal, direction, image, solution, residual_ref, slab_dir, slab_img,
     out1, in1, out2, in2, out_a, in_a, out_b, in_b, out_s, in_s,
     load_sem, gz_send, gz_recv, gx_send, gx_recv,
-    mx_send, mx_recv, mz_send, mz_recv, hop_send, hop_recv,
+    mx_send, mx_recv, mz_send, mz_recv, fz_send, fz_recv, lx_send, lx_recv, hop_send, hop_recv,
 ):
     n = nx * nz
     pairs = diagonal.shape[0]
@@ -48,7 +48,7 @@
     first = first_ref[0]
     my_row = (j - first) & (n - 1)
     my_block = (first + my_row) // n
-    my_col = (first + i) & (n - 1)
+    shift = first & (n - 1)
     odd = (my_block & 1) == 1
 
     def load(a):
@@ -64,7 +64,6 @@
         + lax.broadcasted_iota(jnp.int32, (pairs, CELLS, LANES), 2) // HALF
     )
     owned = (block_of == my_block) | (block_of == my_block + 1)
-    slot_of = lax.broadcasted_iota(jnp.int32, (n, CELLS, LANES), 0)
     left_half = lax.broadcasted_iota(jnp.int32, (order, LANES), 1) < HALF
     even_lanes = (lax.broadcasted_iota(jnp.int32, (CELLS, LANES), 1) < HALF).astype(F32)
     even_mask = even_lanes.astype(BF16)
@@ -73,8 +72,15 @@
     def swap(piece):
         return jnp.where(odd, pltpu.roll(piece, HALF, 1), piece)
 
-    def chosen(slots, which):
-        return jnp.sum(jnp.where(slot_of == which, slots.astype(F32), 0.0), axis=0)
+    def rotated(slots, back):
+        slots = slots.astype(F32)
+        step = 1
+        while step < n:
+            cut = n - step if back else step
+            moved = jnp.concatenate([slots[cut:], slots[:cut]], axis=0)
+            slots = jnp.where((shift & step) != 0, moved, slots)
+            step *= 2
+        return slots.astype(BF16)
 
     def row_copy(src, dst, send, recv, zz, xx):
         return pltpu.make_async_remote_copy(
@@ -91,27 +97,6 @@
     def hop_wait(buf, k, h, slots):
         part = buf.at[pl.ds(0, slots)]
         hop_copy(part, part, k, h, i, j).wait()
-
-    def cross_start(src, dst, k, h, target):
-        def send(step, c):
-            row, col = target(step)
-
-            @pl.when((row != i) | (col != j))
-            def _():
-                hop_copy(src, dst, k, h, row, col).start()
-
-            return c
-
-        lax.fori_loop(0, n, send, 0)
-
-    def cross_wait(buf, k, h):
-        @pl.when(i == j)
-        def _():
-            hop_wait(buf, k, h, n - 1)
-
-        @pl.when(i != j)
-        def _():
-            hop_wait(buf, k, h, n)
 
     def line_start(src, dst, k, h, target):
         def send(step, c):
@@ -163,12 +148,8 @@
 
     def start(k, residual):
         out1[k] = swap(jnp.sum(jnp.where(owned, residual, 0.0), axis=0)).astype(BF16)
-
-        @pl.when(i == j)
-        def _():
-            in1[k, j] = out1[k]
-
-        cross_start(out1.at[k], in1.at[k, j], k, 0, lambda step: ((j + step) % n, i))
+        in1[k, j] = out1[k]
+        line_start(lambda r, c: out1.at[k], in1.at[k, j], k, 0, along_col)
         gathered[k, z, x] = residual[0:live].astype(BF16)
         for dz in range(1, nz):
             spread_z(k, dz).start()
@@ -219,10 +200,10 @@
         forward_z(k, 1)
         if nz > 2:
             forward_z(k, nz - 1)
-        cross_wait(in1.at[k], k, 0)
-        out2[k] = chosen(in1[k], my_col).astype(BF16)
-        in2[k, j] = out2[k]
-        line_start(lambda r, c: out2.at[k], in2.at[k, j], k, 1, along_col)
+        hop_wait(in1.at[k], k, 0, n - 1)
+        out2[k] = rotated(in1[k], False)
+        in2[k, i] = out2[k, i]
+        line_start(lambda r, c: out2.at[k, r], in2.at[k, i], k, 1, along_row)
         for dz in range(2, nz - 1):
             forward_z(k, dz)
         sums_row(k, 0)
@@ -246,7 +227,32 @@
                 mz_send.at[k, chunk, dz - 1], mz_recv.at[k, chunk, dz - 1], zz, x,
             )
 
-        def transposed(chunk, c):
+        def early_z(dz):
+            zz = (z + dz) % nz
+            return row_copy(
+                mirror.at[0, zz], first_z.at[k, dz - 1],
+                fz_send.at[k, dz - 1], fz_recv.at[k, dz - 1], zz, x,
+            )
+
+        def late_x(dx):
+            xx = (x + dx) % nx
+            return row_copy(
+                sums_x.at[xx], last_x.at[k, dx - 1],
+                lx_send.at[k, dx - 1], lx_recv.at[k, dx - 1], z, xx,
+            )
+
+        def pass_x():
+            for dz in range(1, nz):
+                early_z(dz).wait()
+            for xx in range(nx):
+                total = mirror[0, z, xx].astype(F32)
+                for dz in range(1, nz):
+                    total = total + first_z[k, dz - 1, xx].astype(F32)
+                sums_x[xx] = total.astype(BF16)
+            for dx in range(1, nx):
+                late_x(dx).start()
+
+        def transposed(chunk):
             for u in range(per_chunk):
                 p = chunk * per_chunk + u
                 parts = [
@@ -255,11 +261,30 @@
                 ]
                 cells = jnp.transpose(jnp.concatenate(parts, axis=0))
                 mirror[chunk, :, :, u] = cells.astype(BF16).reshape(nz, nx, CELLS, LANES)
+
+        def transposed_x(chunk, c):
+            transposed(chunk)
             for dx in range(1, nx):
                 mirror_x(chunk, dx).start()
             return c
 
-        lax.fori_loop(0, CHUNKS, transposed, 0)
+        transposed(0)
+        for dz in range(1, nz):
+            early_z(dz).start()
+        lax.fori_loop(1, CHUNKS, transposed_x, 0)
+
+        def pass_z(chunk, c):
+            for dx in range(1, nx):
+                mirror_x(chunk, dx).wait()
+            for dz in range(nz):
+                zz = (z + dz) % nz
+                total = mirror[chunk, zz, x].astype(F32)
+                for dx in range(1, nx):
+                    total = total + got_x[k, chunk, dx - 1, zz].astype(F32)
+                sums_z[chunk, zz] = total.astype(BF16)
+            for dz in range(1, nz):
+                mirror_z(chunk, dz).start()
+            return c
 
         norm = sums_end(k, 0)
         beta = jnp.where(k == 0, 0.0, norm / norm_old)
@@ -294,38 +319,23 @@
         rows = jnp.where(left_half, rows[0:order], rows[order:])
 
         out_a[k] = rows.astype(BF16).reshape(n, CELLS, LANES)
-        in_a[k, j] = out_a[k, j]
-        line_start(lambda r, c: out_a.at[k, c], in_a.at[k, j], k, 2, along_col)
+        in_a[k, i] = out_a[k, i]
+        line_start(lambda r, c: out_a.at[k, r], in_a.at[k, i], k, 2, along_row)
         slab_q = rows + beta * slab_img[...]
         slab_img[...] = slab_q
         curve = curve + 2.0 * column_sums((slab_d * slab_q).reshape(n, CELLS, LANES))
         sums_col(k, 2, curve)
 
-        def pass_z(chunk, c):
-            for dx in range(1, nx):
-                mirror_x(chunk, dx).wait()
-            for dz in range(nz):
-                zz = (z + dz) % nz
-                total = mirror[chunk, zz, x].astype(F32)
-                for dx in range(1, nx):
-                    total = total + got_x[k, chunk, dx - 1, zz].astype(F32)
-                sums_z[chunk, zz] = total.astype(BF16)
-            for dz in range(1, nz):
-                mirror_z(chunk, dz).start()
-            return c
-
-        lax.fori_loop(0, CHUNKS // 2, pass_z, 0)
+        pass_x()
+        pass_z(1, 0)
+        pass_z(2, 0)
 
         hop_wait(in_a.at[k], k, 2, n - 1)
-        out_b[k] = jnp.sum(in_a[k].astype(F32), axis=0).astype(BF16)
-
-        @pl.when(i == j)
-        def _():
-            in_b[k, i] = out_b[k]
-
-        cross_start(out_b.at[k], in_b.at[k, i], k, 3, lambda step: (j, (i + step) % n))
+        out_b[k] = rotated(in_a[k], True)
+        in_b[k, j] = out_b[k, j]
+        line_start(lambda r, c: out_b.at[k, c], in_b.at[k, j], k, 3, along_col)
         sums_row(k, 2)
-        lax.fori_loop(CHUNKS // 2, CHUNKS, pass_z, 0)
+        pass_z(3, 0)
 
         def finish_z(chunk, c):
             for dz in range(1, nz):
@@ -338,11 +348,17 @@
             return c
 
         image[...] = beta_cell * image[...] + diagonal[...] * residual
-        lax.fori_loop(0, CHUNKS, finish_z, 0)
+        lax.fori_loop(1, CHUNKS, finish_z, 0)
+        for dx in range(1, nx):
+            late_x(dx).wait()
+        total = sums_x[x].astype(F32)
+        for dx in range(1, nx):
+            total = total + last_x[k, dx - 1].astype(F32)
+        image[0:per_chunk] = image[0:per_chunk] + total
         applied = image[...]
 
-        cross_wait(in_b.at[k], k, 3)
-        piece = swap(chosen(in_b[k], my_row))
+        hop_wait(in_b.at[k], k, 3, n - 1)
+        piece = swap(jnp.sum(in_b[k].astype(F32), axis=0))
         applied = applied + jnp.where(owned, piece.reshape(1, CELLS, LANES), 0.0)
         image[...] = applied
         length = (norm / sums_end(k, 2)).reshape(1, 1, LANES)
@@ -399,6 +415,9 @@
                 pltpu.VMEM((ITERS, CHUNKS, nx - 1, nz) + part, BF16),
                 pltpu.VMEM((CHUNKS, nz) + part, BF16),
                 pltpu.VMEM((ITERS, CHUNKS, nz - 1) + part, BF16),
+                pltpu.VMEM((ITERS, nz - 1, nx) + part, BF16),
+                pltpu.VMEM((nx,) + part, BF16),
+                pltpu.VMEM((ITERS, nx - 1) + part, BF16),
                 pltpu.VMEM(vec, F32),
                 pltpu.VMEM(vec, F32),
                 pltpu.VMEM(vec, F32),
@@ -408,11 +427,11 @@
                 pltpu.VMEM((order, LANES), F32),
                 pltpu.VMEM((ITERS,) + piece, BF16),
                 pltpu.VMEM((ITERS, n) + piece, BF16),
-                pltpu.VMEM((ITERS,) + piece, BF16),
-                pltpu.VMEM((ITERS, n) + piece, BF16),
-                pltpu.VMEM((ITERS, n) + piece, BF16),
-                pltpu.VMEM((ITERS, n) + piece, BF16),
-                pltpu.VMEM((ITERS,) + piece, BF16),
+                pltpu.VMEM((ITERS, n) + piece, BF16),
+                pltpu.VMEM((ITERS, n) + piece, BF16),
+                pltpu.VMEM((ITERS, n) + piece, BF16),
+                pltpu.VMEM((ITERS, n) + piece, BF16),
+                pltpu.VMEM((ITERS, n) + piece, BF16),
                 pltpu.VMEM((ITERS, n) + piece, BF16),
                 pltpu.VMEM((ITERS, 4, 1, LANES), F32),
                 pltpu.VMEM((ITERS, 4, n, 1, LANES), F32),
@@ -425,6 +444,10 @@
                 dma((ITERS, CHUNKS, nx - 1)),
                 dma((ITERS, CHUNKS, nz - 1)),
                 dma((ITERS, CHUNKS, nz - 1)),
+                dma((ITERS, nz - 1)),
+                dma((ITERS, nz - 1)),
+                dma((ITERS, nx - 1)),
+                dma((ITERS, nx - 1)),
                 dma((ITERS, 8)),
                 dma((ITERS, 8)),
             ],

time: 112 us -> 107 us (0.955); the launches traced: 112 us -> 106 us
  Pallas kernels: 109 us -> 103 us
    pallas_call x1, Pallas kernels: 109 us -> 103 us  [solve(): pl.pallas_call(functools.partial(kernel, nx, nz, live), out_shape=[jax.Sh...]
where the time goes in v4:
time: 107 us; the launch traced here: 106 us
  Pallas kernels  103 us (96%)
  local copies, waits for them, and re-layouts  1.45 us (1%)
  between operations  1.33 us (1%)
    pallas_call x1, Pallas kernels, solve(): pl.pallas_call(functools.partial(kernel, nx, nz, live), out_shape=[jax.Sh...  103 us

profile of v4, /device:TPU:1, one launch (start us, length us, event | category | flops | bytes accessed | tf_op | source)
XLA Modules:
  0.0 105.9 jit_solution(14962729668797889945)
XLA Ops:
  1.3 103.1 %conditional.1 = ((f32[16,40,64]{2,1,0:T(8,128)S(1)}, f32[16,40,64]{2,1,0:T(8,128)S(1)})) conditional(s32[]{:T(128)} %clamp.3, (s32[1]{0:T(128)}, bf16[2,256,40,256]{3,2,1,0:T(8,128)(2,1)}, f32[16,40]{1,0:T(8,128)}, f32[16,40,64]{2,1,0:T(8,128)}) %tuple.22, (s32[1]{0:T(128)}, bf16[2,256,40,256]{3,2,1,0:T(8,128)(2,1)}, ...), branch_computations={%region_0.1_spmd, %region_1.2_spmd, %region_2.3_spmd, %region_3.4_... | conditional | bytes 8 | solution.py:463
  1.3 102.9 %conjugate_gradients_8.1 = (f32[16,40,64]{2,1,0:T(8,128)S(1)}, f32[16,40,64]{2,1,0:T(8,128)S(1)}) custom-call(s32[1]{0:T(128)} %get-tuple-element.44.first_ref, bf16[2,256,40,256]{3,2,1,0:T(8,128)(2,1)} %get-tuple-element.90.matrix_hbm, f32[16,40]{1,0:T(8,128)} %get-tuple-element.95.diag_ref, f32[16,40,64]{2,1,0:T(8,128)} %get-tuple-element.100.right_ref), custom_call_target="tpu_custom_call" | custom-call | tf_op jit(solution)/shard_map/cond/branch_1_fun/conjugate_gradients_8/pallas_call | solution.py:400
  104.5 0.7 copy.44
  105.2 0.7 copy.45

commit v5 on v4

--- a/solution.py
+++ b/solution.py
@@ -51,6 +51,15 @@
     shift = first & (n - 1)
     odd = (my_block & 1) == 1
 
+    barrier = pltpu.get_barrier_semaphore()
+
+    def greet(step, c):
+        for device in (((i + step) % n, j), (i, (j + step) % n)):
+            pl.semaphore_signal(barrier, inc=1, device_id=device, device_id_type=MESH)
+        return c
+
+    lax.fori_loop(1, n, greet, 0)
+
     def load(a):
         return pltpu.make_async_copy(
             matrix_hbm.at[a, :, pl.ds(0, stored)], raw.at[a], load_sem.at[a]
@@ -112,21 +121,15 @@
     def along_row(step):
         return (i + step) % n, j
 
-    def sums_col(k, h, value):
+    def sums_start(k, h, value, along):
         out_s[k, h] = value
-        in_s[k, h, j] = value
-        line_start(lambda r, c: out_s.at[k, h], in_s.at[k, h, j], k, 4 + h, along_col)
-
-    def sums_row(k, h):
+        place = j if along is along_col else i
+        in_s[k, h, place] = value
+        line_start(lambda r, c: out_s.at[k, h], in_s.at[k, h, place], k, 4 + h, along)
+
+    def sums_end(k, h):
         hop_wait(in_s.at[k, h], k, 4 + h, n - 1)
-        value = jnp.sum(in_s[k, h], axis=0)
-        out_s[k, h + 1] = value
-        in_s[k, h + 1, i] = value
-        line_start(lambda r, c: out_s.at[k, h + 1], in_s.at[k, h + 1, i], k, 5 + h, along_row)
-
-    def sums_end(k, h):
-        hop_wait(in_s.at[k, h + 1], k, 5 + h, n - 1)
-        return jnp.sum(in_s[k, h + 1], axis=0)
+        return jnp.sum(in_s[k, h], axis=0)
 
     def spread_z(k, dz):
         return row_copy(
@@ -155,7 +158,7 @@
             spread_z(k, dz).start()
         for dx in range(1, nx):
             spread_x(k, dx, 0).start()
-        sums_col(k, 0, column_sums(residual * residual))
+        sums_start(k, 0, column_sums(residual * residual), along_col)
 
     for tile in range(2 * pairs // 8):
         values = jnp.swapaxes(right_ref[:, tile * 8 : tile * 8 + 8, :], 0, 1)
@@ -174,6 +177,7 @@
     image[...] = jnp.zeros_like(image)
     slab_dir[...] = jnp.zeros_like(slab_dir)
     slab_img[...] = jnp.zeros_like(slab_img)
+    pl.semaphore_wait(barrier, 2 * (n - 1))
     start(0, residual_ref[...])
 
     for a in range(block_rows):
@@ -206,7 +210,7 @@
         line_start(lambda r, c: out2.at[k, r], in2.at[k, i], k, 1, along_row)
         for dz in range(2, nz - 1):
             forward_z(k, dz)
-        sums_row(k, 0)
+        sums_start(k, 1, sums_end(k, 0), along_row)
         hop_wait(in2.at[k], k, 1, n - 1)
         slab = in2[k].astype(F32).reshape(order, LANES)
 
@@ -286,7 +290,7 @@
                 mirror_z(chunk, dz).start()
             return c
 
-        norm = sums_end(k, 0)
+        norm = sums_end(k, 1)
         beta = jnp.where(k == 0, 0.0, norm / norm_old)
         slab_d = slab + beta * slab_dir[...]
         slab_dir[...] = slab_d
@@ -324,7 +328,7 @@
         slab_q = rows + beta * slab_img[...]
         slab_img[...] = slab_q
         curve = curve + 2.0 * column_sums((slab_d * slab_q).reshape(n, CELLS, LANES))
-        sums_col(k, 2, curve)
+        sums_start(k, 2, curve, along_row)
 
         pass_x()
         pass_z(1, 0)
@@ -334,7 +338,7 @@
         out_b[k] = rotated(in_a[k], True)
         in_b[k, j] = out_b[k, j]
         line_start(lambda r, c: out_b.at[k, c], in_b.at[k, j], k, 3, along_col)
-        sums_row(k, 2)
+        sums_start(k, 3, sums_end(k, 2), along_col)
         pass_z(3, 0)
 
         def finish_z(chunk, c):
@@ -361,8 +365,7 @@
         piece = swap(jnp.sum(in_b[k].astype(F32), axis=0))
         applied = applied + jnp.where(owned, piece.reshape(1, CELLS, LANES), 0.0)
         image[...] = applied
-        length = (norm / sums_end(k, 2)).reshape(1, 1, LANES)
-        solution[...] = solution[...] + length * cells_d
+        length = (norm / sums_end(k, 3)).reshape(1, 1, LANES)
         residual = residual - length * applied
         residual_ref[...] = residual
 
@@ -370,6 +373,7 @@
         def _():
             start(k + 1, residual)
 
+        solution[...] = solution[...] + length * cells_d
         return norm
 
     lax.fori_loop(0, ITERS, iteration, jnp.ones((1, LANES), F32))
@@ -452,7 +456,9 @@
                 dma((ITERS, 8)),
             ],
             compiler_params=pltpu.CompilerParams(
-                has_side_effects=True, vmem_limit_bytes=56 * 1024 * 1024
+                collective_id=live // CHUNKS,
+                has_side_effects=True,
+                vmem_limit_bytes=56 * 1024 * 1024,
             ),
             name=f"conjugate_gradients_{live}",
         )(slab_first, matrix, diagonal, right_side)

time: 107 us -> 97 us (0.907)
  Pallas kernels: 103 us -> 93.7 us
    pallas_call x1, Pallas kernels: 103 us -> 93.7 us  [solve(): pl.pallas_call(functools.partial(kernel, nx, nz, live), out_shape=[jax.Sh...]
where the time goes in v5:
time: 97 us; the launch traced here: 96.7 us
  Pallas kernels  93.7 us (97%)
  local copies, waits for them, and re-layouts  1.45 us (1%)
  between operations  1.33 us (1%)
    pallas_call x1, Pallas kernels, solve(): pl.pallas_call(functools.partial(kernel, nx, nz, live), out_shape=[jax.Sh...  93.7 us

profile of v5, /device:TPU:1, one launch (start us, length us, event | category | flops | bytes accessed | tf_op | source)
XLA Modules:
  0.0 96.7 jit_solution(14733124618285366156)
XLA Ops:
  1.3 93.9 %conditional.1 = ((f32[16,40,64]{2,1,0:T(8,128)S(1)}, f32[16,40,64]{2,1,0:T(8,128)S(1)})) conditional(s32[]{:T(128)} %clamp.3, (s32[1]{0:T(128)}, bf16[2,256,40,256]{3,2,1,0:T(8,128)(2,1)}, f32[16,40]{1,0:T(8,128)}, f32[16,40,64]{2,1,0:T(8,128)}) %tuple.22, (s32[1]{0:T(128)}, bf16[2,256,40,256]{3,2,1,0:T(8,128)(2,1)}, ...), branch_computations={%region_0.1_spmd, %region_1.2_spmd, %region_2.3_spmd, %region_3.4_... | conditional | bytes 8 | solution.py:469
  1.3 93.7 %conjugate_gradients_8.1 = (f32[16,40,64]{2,1,0:T(8,128)S(1)}, f32[16,40,64]{2,1,0:T(8,128)S(1)}) custom-call(s32[1]{0:T(128)} %get-tuple-element.44.first_ref, bf16[2,256,40,256]{3,2,1,0:T(8,128)(2,1)} %get-tuple-element.90.matrix_hbm, f32[16,40]{1,0:T(8,128)} %get-tuple-element.95.diag_ref, f32[16,40,64]{2,1,0:T(8,128)} %get-tuple-element.100.right_ref), custom_call_target="tpu_custom_call" | custom-call | tf_op jit(solution)/shard_map/cond/branch_1_fun/conjugate_gradients_8/pallas_call | solution.py:404
  95.3 0.7 copy.44
  96.0 0.7 copy.45
